TPU v7x, 32 devices: a whole 2x2x4 slice. The times are simulated.
32 devices in a mesh: dp: 16 (over z, x, core), tensor: 2 (over y).
Axes of the slice: x: 2, y: 2, z: 4, core: 2. Of those that a mesh axis runs over, the one named last changes fastest.
Arguments:
- inputs: bfloat16 [16384, 1024], P(('dp', 'tensor')), may hold values from -6 to 6
- norm1_gain: float32 [1024], replicated, may hold values from 0.5 to 1.5
- norm1_bias: float32 [1024], replicated, may hold values from -3 to 3
- qkv_weight: bfloat16 [1024, 3072], P('dp', 'tensor'), may hold values from -0.25 to 0.25
- qv_bias: float32 [2, 1024], P(None, 'tensor'), may hold values from -1.2 to 1.2
- out_weight: bfloat16 [1024, 1024], P('tensor', 'dp'), may hold values from -0.75 to 0.75
- out_bias: float32 [1024], replicated, may hold values from -3 to 3
- norm2_gain: float32 [1024], replicated, may hold values from 0.5 to 1.5
- norm2_bias: float32 [1024], replicated, may hold values from -3 to 3
- fc1_weight: bfloat16 [1024, 4096], P('dp', 'tensor'), may hold values from -0.1875 to 0.1875
- fc1_bias: float32 [4096], P('tensor'), may hold values from -3 to 3
- fc2_weight: bfloat16 [4096, 1024], P('tensor', 'dp'), may hold values from -0.09375 to 0.09375
- fc2_bias: float32 [1024], replicated, may hold values from -3 to 3
- cotangent: bfloat16 [16384, 1024], P(('dp', 'tensor')), may hold values from -6 to 6
Outputs:
- outputs: bfloat16 [16384, 1024], P(('dp', 'tensor'))
- grad_inputs: float32 [16384, 1024], P(('dp', 'tensor'))
- grad_norm1_gain: float32 [1024], replicated
- grad_norm1_bias: float32 [1024], replicated
- grad_qkv_weight: float32 [1024, 3072], P('dp', 'tensor')
- grad_qv_bias: float32 [2, 1024], P(None, 'tensor')
- grad_out_weight: float32 [1024, 1024], P('tensor', 'dp')
- grad_out_bias: float32 [1024], replicated
- grad_norm2_gain: float32 [1024], replicated
- grad_norm2_bias: float32 [1024], replicated
- grad_fc1_weight: float32 [1024, 4096], P('dp', 'tensor')
- grad_fc1_bias: float32 [4096], P('tensor')
- grad_fc2_weight: float32 [4096, 1024], P('tensor', 'dp')
- grad_fc2_bias: float32 [1024], replicated
All inputs are finite; a program needn't handle non-finite values.
Results may differ from a plain program's by a relative error of at most 0.012.
The roundings to bfloat16 on the way count: a program that leaves them out, or rounds other values in their place, can miss the bound.
Values may be sent and summed in bfloat16 or wider, within the bound.
A program may use at most 192 MiB of HBM per device.

v0:
```python
from functools import partial

import jax
import jax.numpy as jnp
from jax import lax
from jax.sharding import PartitionSpec as P

D = 1024
HD = 64
FF = 4096
LEN = 1024
SEQS = 1


EPS = 1e-05


def layer_norm(values, gain, shift):
    center = values - jnp.mean(values, -1, keepdims=True)
    spread = jnp.mean(center * center, -1, keepdims=True)
    return center * lax.rsqrt(spread + EPS) * gain + shift


def masked_scores(query_block, keys, first_row, factor):
    block_rows = query_block.shape[0]
    scores = (
        jnp.einsum("qhd,khd->hqk", query_block, keys, preferred_element_type=jnp.float32) * factor
    )
    query_pos = first_row + jnp.arange(block_rows, dtype=jnp.int32)
    key_pos = jnp.arange(keys.shape[0], dtype=jnp.int32)
    allowed = key_pos[None, :] <= query_pos[:, None]
    return jnp.where(allowed[None], scores, -1e30)


def attention_forward(queries, keys, values, factor):
    length = queries.shape[0]
    block_rows = min(512, length)
    block_count = length // block_rows

    def one_block(block_index):
        first_row = block_index * block_rows
        query_block = lax.dynamic_slice_in_dim(queries, first_row, block_rows, 0)
        scores = masked_scores(query_block, keys, first_row, factor)
        row_max = jnp.max(scores, -1, keepdims=True)
        expo = jnp.exp(scores - row_max)
        exp_total = jnp.sum(expo, -1, keepdims=True)
        probs_low = (expo / exp_total).astype(jnp.bfloat16)
        context = jnp.einsum("hqk,khd->qhd", probs_low, values, preferred_element_type=jnp.float32)
        return (context.astype(jnp.bfloat16), (row_max + jnp.log(exp_total))[..., 0])

    context, log_total = lax.map(one_block, jnp.arange(block_count, dtype=jnp.int32))
    return (context.reshape(queries.shape), log_total)


def attention_backward(queries, keys, values, log_total, grad_context, factor):
    length = queries.shape[0]
    block_rows = min(512, length)
    block_count = length // block_rows

    def one_block(carry, block_index):
        grad_keys, grad_values = carry
        first_row = block_index * block_rows
        query_block = lax.dynamic_slice_in_dim(queries, first_row, block_rows, 0)
        grad_block = lax.dynamic_slice_in_dim(grad_context, first_row, block_rows, 0)
        scores = masked_scores(query_block, keys, first_row, factor)
        probs = jnp.exp(scores - log_total[block_index][..., None])
        probs_low = probs.astype(jnp.bfloat16)
        grad_values = grad_values + jnp.einsum(
            "hqk,qhd->khd", probs_low, grad_block, preferred_element_type=jnp.float32
        )
        grad_probs = jnp.einsum(
            "qhd,khd->hqk", grad_block, values, preferred_element_type=jnp.float32
        )
        grad_scores = probs * (grad_probs - jnp.sum(probs * grad_probs, -1, keepdims=True))
        grad_scores = grad_scores.astype(jnp.bfloat16)
        grad_query = (
            jnp.einsum("hqk,khd->qhd", grad_scores, keys, preferred_element_type=jnp.float32)
            * factor
        )
        grad_keys = (
            grad_keys
            + jnp.einsum(
                "hqk,qhd->khd", grad_scores, query_block, preferred_element_type=jnp.float32
            )
            * factor
        )
        return ((grad_keys, grad_values), grad_query.astype(jnp.bfloat16))

    start_carry = (jnp.zeros(keys.shape, jnp.float32), jnp.zeros(values.shape, jnp.float32))
    (grad_keys, grad_values), grad_queries = lax.scan(
        one_block, start_carry, jnp.arange(block_count, dtype=jnp.int32)
    )
    return (
        grad_queries.reshape(queries.shape),
        grad_keys.astype(jnp.bfloat16),
        grad_values.astype(jnp.bfloat16),
    )


def row_product(left_rows, right_mat):
    return jnp.dot(left_rows, right_mat, preferred_element_type=jnp.float32)


def row_product_back(left_rows, right_mat):
    return jnp.einsum("rc,dc->rd", left_rows, right_mat, preferred_element_type=jnp.float32)


def body(
    inputs,
    norm1_gain,
    norm1_bias,
    qkv_weight,
    qv_bias,
    out_weight,
    out_bias,
    norm2_gain,
    norm2_bias,
    fc1_weight,
    fc1_bias,
    fc2_weight,
    fc2_bias,
    cotangent,
):
    width_here = qv_bias.shape[1]
    heads_here = width_here // HD
    hidden_here = fc1_bias.shape[0]
    factor = HD ** (-0.5)
    inputs_f = inputs.astype(jnp.float32)
    tensor_index = lax.axis_index("tensor")
    qkv_full, out_full, fc1_full, fc2_full = (
        lax.all_gather(qkv_weight, "dp", axis=0, tiled=True),
        lax.all_gather(out_weight, "dp", axis=1, tiled=True),
        lax.all_gather(fc1_weight, "dp", axis=0, tiled=True),
        lax.all_gather(fc2_weight, "dp", axis=1, tiled=True),
    )
    normed1 = lax.all_gather(
        layer_norm(inputs_f, norm1_gain, norm1_bias).astype(jnp.bfloat16),
        "tensor",
        axis=0,
        tiled=True,
    )
    total_rows = normed1.shape[0]
    no_bias = jnp.zeros((heads_here, HD), jnp.float32)
    head_bias = jnp.stack(
        [qv_bias[0].reshape(heads_here, HD), no_bias, qv_bias[1].reshape(heads_here, HD)], 1
    )
    projected = (
        jnp.dot(normed1, qkv_full, preferred_element_type=jnp.float32).reshape(
            total_rows, heads_here, 3, HD
        )
        + head_bias
    )
    projected = projected.astype(jnp.bfloat16).reshape(SEQS, LEN, heads_here, 3, HD)
    queries = projected[:, :, :, 0]
    keys = projected[:, :, :, 1]
    values = projected[:, :, :, 2]
    context, log_total = lax.map(
        lambda operand: attention_forward(operand[0], operand[1], operand[2], factor),
        (queries, keys, values),
    )
    context = context.reshape(total_rows, width_here)
    attn_part = lax.psum_scatter(
        row_product(context, out_full), "tensor", scatter_dimension=0, tiled=True
    )
    middle = inputs_f + attn_part + out_bias
    normed2 = lax.all_gather(
        layer_norm(middle, norm2_gain, norm2_bias).astype(jnp.bfloat16),
        "tensor",
        axis=0,
        tiled=True,
    )
    pre_act = jnp.dot(normed2, fc1_full, preferred_element_type=jnp.float32) + fc1_bias
    activ = jax.nn.gelu(pre_act, approximate=True).astype(jnp.bfloat16)
    branch = lax.psum_scatter(
        row_product(activ, fc2_full).astype(jnp.bfloat16), "tensor", scatter_dimension=0, tiled=True
    ).astype(jnp.float32)
    outputs = (middle + branch + fc2_bias).astype(jnp.bfloat16)
    qkv_back, out_back, fc1_back, fc2_back = (
        lax.all_gather(qkv_weight, "dp", axis=0, tiled=True),
        lax.all_gather(out_weight, "dp", axis=1, tiled=True),
        lax.all_gather(fc1_weight, "dp", axis=0, tiled=True),
        lax.all_gather(fc2_weight, "dp", axis=1, tiled=True),
    )
    grad_outputs = cotangent.astype(jnp.float32)
    grad_branch = lax.all_gather(cotangent, "tensor", axis=0, tiled=True)
    grad_activ = jnp.einsum("rd,fd->rf", grad_branch, fc2_back, preferred_element_type=jnp.float32)
    grad_fc2 = jnp.einsum("rf,rd->fd", activ, grad_branch, preferred_element_type=jnp.float32)
    gelu_pull = jax.vjp(partial(jax.nn.gelu, approximate=True), pre_act)[1]
    grad_pre = gelu_pull(grad_activ)[0].astype(jnp.bfloat16)
    grad_fc1_b = jnp.sum(grad_pre.astype(jnp.float32), 0)
    grad_fc1 = jnp.einsum("rd,rf->df", normed2, grad_pre, preferred_element_type=jnp.float32)
    grad_normed2 = lax.psum_scatter(
        row_product_back(grad_pre, fc1_back), "tensor", scatter_dimension=0, tiled=True
    )
    norm2_pull = jax.vjp(layer_norm, middle, norm2_gain, norm2_bias)[1]
    grad_mid_norm, grad_gain2, grad_shift2 = norm2_pull(grad_normed2)
    grad_middle = grad_outputs + grad_mid_norm
    grad_attn = lax.all_gather(grad_middle.astype(jnp.bfloat16), "tensor", axis=0, tiled=True)
    grad_ctx = jnp.einsum(
        "rd,cd->rc", grad_attn, out_back, preferred_element_type=jnp.float32
    ).astype(jnp.bfloat16)
    grad_out_w = jnp.einsum("rc,rd->cd", context, grad_attn, preferred_element_type=jnp.float32)
    grad_queries, grad_keys, grad_values = lax.map(
        lambda operand: attention_backward(
            operand[0], operand[1], operand[2], operand[3], operand[4], factor
        ),
        (queries, keys, values, log_total, grad_ctx.reshape(SEQS, LEN, heads_here, HD)),
    )
    grad_proj = jnp.stack([grad_queries, grad_keys, grad_values], 3).reshape(
        total_rows, 3 * width_here
    )
    grad_qv_here = jnp.stack(
        [
            jnp.sum(grad_queries.astype(jnp.float32), (0, 1)).reshape(width_here),
            jnp.sum(grad_values.astype(jnp.float32), (0, 1)).reshape(width_here),
        ]
    )
    grad_qkv_w = jnp.einsum("rd,rc->dc", normed1, grad_proj, preferred_element_type=jnp.float32)
    grad_normed1 = lax.psum_scatter(
        row_product_back(grad_proj, qkv_back), "tensor", scatter_dimension=0, tiled=True
    )
    norm1_pull = jax.vjp(layer_norm, inputs_f, norm1_gain, norm1_bias)[1]
    grad_in_norm, grad_gain1, grad_shift1 = norm1_pull(grad_normed1)
    grad_inputs = grad_middle + grad_in_norm
    grad_qkv_s, grad_out_s, grad_fc1_s, grad_fc2_s = (
        lax.psum_scatter(grad_qkv_w, "dp", scatter_dimension=0, tiled=True),
        lax.psum_scatter(grad_out_w, "dp", scatter_dimension=1, tiled=True),
        lax.psum_scatter(grad_fc1, "dp", scatter_dimension=0, tiled=True),
        lax.psum_scatter(grad_fc2, "dp", scatter_dimension=1, tiled=True),
    )
    vector_terms = jnp.stack(
        [
            grad_gain1,
            grad_shift1,
            grad_gain2,
            grad_shift2,
            jnp.sum(grad_middle, 0),
            jnp.sum(grad_outputs, 0),
        ]
    )
    qv_whole = lax.dynamic_update_slice_in_dim(
        jnp.zeros((2, D), jnp.float32), grad_qv_here, tensor_index * width_here, 1
    )
    fc1_whole = lax.dynamic_update_slice_in_dim(
        jnp.zeros((FF,), jnp.float32), grad_fc1_b, tensor_index * hidden_here, 0
    )
    vector_sum, qv_sum, fc1_sum = lax.psum((vector_terms, qv_whole, fc1_whole), ("dp", "tensor"))
    grad_qv = lax.dynamic_slice_in_dim(qv_sum, tensor_index * width_here, width_here, 1)
    grad_fc1_bias = lax.dynamic_slice_in_dim(fc1_sum, tensor_index * hidden_here, hidden_here, 0)
    return (
        outputs,
        grad_inputs,
        vector_sum[0],
        vector_sum[1],
        grad_qkv_s,
        grad_qv,
        grad_out_s,
        vector_sum[4],
        vector_sum[2],
        vector_sum[3],
        grad_fc1_s,
        grad_fc1_bias,
        grad_fc2_s,
        vector_sum[5],
    )


def solution(mesh):
    placed = (
        P(("dp", "tensor"), None),
        P(),
        P(),
        P("dp", "tensor"),
        P(None, "tensor"),
        P("tensor", "dp"),
        P(),
        P(),
        P(),
        P("dp", "tensor"),
        P("tensor"),
        P("tensor", "dp"),
        P(),
        P(("dp", "tensor"), None),
    )
    return jax.shard_map(
        body,
        mesh=mesh,
        in_specs=placed,
        out_specs=(
            P(("dp", "tensor"), None),
            P(("dp", "tensor"), None),
            P(),
            P(),
            P("dp", "tensor"),
            P(None, "tensor"),
            P("tensor", "dp"),
            P(),
            P(),
            P(),
            P("dp", "tensor"),
            P("tensor"),
            P("tensor", "dp"),
            P(),
        ),
        check_vma=False,
    )
```

profile of v0, /device:TPU:0, one launch (start us, length us, event | category | flops | bytes accessed | tf_op | source)
XLA Modules:
  0.0 1065.8 jit_solution(17396754995898361788)
XLA Ops:
  14.9 34.1 %all-gather.9.cloned.1.call-done = bf16[1024,1024]{1,0:T(8,128)(2,1)} async-done(((bf16[512,1024]{1,0:T(8,128)(2,1)}), bf16[1024,1024]{1,0:T(8,128)(2,1)}) %all-gather.9.cloned.1.call-update) | async-done | bytes 2097168 | tf_op jit(solution)/shard_map/all_gather | solution.py:136
  49.0 47.5 %all-gather.11.cloned.1.call-done = bf16[1024,1536]{1,0:T(8,128)(2,1)} async-done(((bf16[64,1536]{1,0:T(8,128)(2,1)}), bf16[1024,1536]{1,0:T(8,128)(2,1)}) %all-gather.11.cloned.1.call-update) | async-done | bytes 3145744 | tf_op jit(solution)/shard_map/all_gather | solution.py:131
  104.6 31.0 %while.47 = (s32[]{:T(128)}, bf16[2,512,8,64]{1,3,2,0:T(8,128)(2,1)S(1)}, f32[2,8,512]{2,1,0:T(8,128)S(1)}, s32[2]{0:T(128)S(1)}, bf16[1024,8,64]{0,2,1:T(8,128)...) while((s32[]{:T(128)}, ...), condition=%wide.region_5.6_spmd, body=%wide.region_2.5_spmd.sunk | while | flops 1124856320 | bytes 55709888 | solution.py:51
  143.1 52.6 %reduce-scatter.9.cloned.1.call-done = f32[512,1024]{1,0:T(8,128)} async-done(((f32[1024,1024]{1,0:T(8,128)}), f32[512,1024]{1,0:T(8,128)}) %reduce-scatter.9.cloned.1.call-update) | async-done | bytes 2097168 | tf_op jit(solution)/shard_map/reduce_scatter | solution.py:162
  202.2 46.3 %all-gather.17.cloned.1.call-done = bf16[1024,2048]{1,0:T(8,128)(2,1)} async-done(((bf16[64,2048]{1,0:T(8,128)(2,1)}), bf16[1024,2048]{1,0:T(8,128)(2,1)}) %all-gather.17.cloned.1.call-update) | async-done | bytes 4194320 | tf_op jit(solution)/shard_map/all_gather | solution.py:133
  248.5 33.7 %all-gather.15.cloned.1.call-done = bf16[1024,1024]{1,0:T(8,128)(2,1)} async-done(((bf16[512,1024]{1,0:T(8,128)(2,1)}), bf16[1024,1024]{1,0:T(8,128)(2,1)}) %all-gather.15.cloned.1.call-update) | async-done | bytes 2097168 | tf_op jit(solution)/shard_map/all_gather | solution.py:166
  282.2 10.9 %fusion.60 = f32[1024,2048]{1,0:T(8,128)} fusion(bf16[1024,1024]{1,0:T(8,128)(2,1)} %all-gather.15.cloned.1.call-done, bf16[1024,2048]{1,0:T(8,128)(2,1)} %all-gather.17.cloned.1.call-done), kind=kOutput, calls=%fused_computation.112 | convolution fusion | flops 4294967296 | bytes 14680064 | tf_op jit(solution)/shard_map/dot_general | solution.py:172
  293.1 23.9 %all-gather.21.cloned.1.call-done = bf16[1024,1024]{1,0:T(8,128)(2,1)} async-done(((bf16[512,1024]{1,0:T(8,128)(2,1)}), bf16[1024,1024]{1,0:T(8,128)(2,1)}) %all-gather.21.cloned.1.call-update) | async-done | bytes 2097168 | tf_op jit(solution)/shard_map/all_gather | solution.py:185
  317.0 53.0 %all-gather.19.cloned.1.call-done = bf16[2048,1024]{0,1:T(8,128)(2,1)} async-done(((bf16[2048,64]{0,1:T(8,128)(2,1)}), bf16[2048,1024]{0,1:T(8,128)(2,1)}) %all-gather.19.cloned.1.call-update) | async-done | bytes 4194320 | tf_op jit(solution)/shard_map/all_gather | solution.py:134
  370.0 13.7 %convert_reduce_fusion = (f32[2048]{0:T(1024)}, bf16[1024,2048]{1,0:T(8,128)(2,1)S(1)}) fusion(f32[1024,2048]{1,0:T(8,128)} %fusion.60, f32[2048]{0:T(1024)S(1)} %copy-done.42, bf16[1024,1024]{1,0:T(8,128)(2,1)} %all-gather.21.cloned.1.call-done, bf16[2048,1024]{0,1:T(8,128)(2,1)} %all-gather.19.cloned.1.call-done), kind=kOutput, calls=%fused_computation.49 | convolution fusion | flops 4343199744 | bytes 18890752 | tf_op jit(solution)/shard_map/rd,fd->rf/dot_general | solution.py:186
  392.4 11.8 %convolution_convert_fusion = bf16[1024,1024]{1,0:T(8,128)(2,1)} fusion(bf16[2048,1024]{0,1:T(8,128)(2,1)} %all-gather.19.cloned.1.call-done, f32[1024,2048]{1,0:T(8,128)} %fusion.60, f32[2048]{0:T(1024)S(1)} %copy-done.42), kind=kOutput, calls=%fused_computation.80 | convolution fusion | flops 4316987392 | bytes 14688256 | tf_op jit(solution)/shard_map/dot_general | solution.py:101
  404.3 40.6 %reduce-scatter.13.cloned.1.call-done = f32[512,1024]{1,0:T(8,128)} async-done(((f32[1024,1024]{1,0:T(8,128)}), f32[512,1024]{1,0:T(8,128)}) %reduce-scatter.13.cloned.1.call-update) | async-done | bytes 2097168 | tf_op jit(solution)/shard_map/reduce_scatter | solution.py:192
  448.5 30.3 %reduce-scatter.11.cloned.1.call-done = bf16[512,1024]{1,0:T(8,128)(2,1)} async-done(((bf16[1024,1024]{1,0:T(8,128)(2,1)}), bf16[512,1024]{1,0:T(8,128)(2,1)}) %reduce-scatter.11.cloned.1.call-update) | async-done | bytes 1048592 | tf_op jit(solution)/shard_map/reduce_scatter | solution.py:174
  485.8 33.2 %all-gather.23.cloned.1.call-done = bf16[1024,1024]{1,0:T(8,128)(2,1)} async-done(((bf16[512,1024]{1,0:T(8,128)(2,1)}), bf16[1024,1024]{1,0:T(8,128)(2,1)}) %all-gather.23.cloned.1.call-update) | async-done | bytes 2097168 | tf_op jit(solution)/shard_map/all_gather | solution.py:198
  524.3 92.3 %while.48 = (s32[]{:T(128)}, f32[1024,8,64]{0,2,1:T(8,128)}, f32[1024,8,64]{0,2,1:T(8,128)}, bf16[2,512,8,64]{1,3,2,0:T(8,128)(2,1)}, s32[2]{0:T(128)S(1)}, /*in...) while((s32[]{:T(128)}, f32[1024,8,64]{0,2,1:T(8,128)}, ...), condition=%wide.region_15.16_spmd.clone, body=%wide.region_13.15_spmd.clone.sunk | while | flops 2725769728 | bytes 212685392 | solution.py:90
  533.3 11.4 %multiply_reduce_fusion.5 = (f32[8,512]{1,0:T(8,128)}, f32[8,512,1024]{2,1,0:T(8,128)}) fusion(f32[8,512,1024]{2,1,0:T(8,128)S(1)} %fusion.125, f32[8,512]{1,0:T(8,128)} %dynamic-slice_bitcast_fusion.2, bf16[1024,8,64]{0,2,1:T(8,128)(2,1)S(1)} %get-tuple-element.441, bf16[1024,8,64]{0,2,1:T(8,128)(2,1)} %get-tuple-element.440, s32[]{:T(128)S(6)} %select_n.57, ...), kind=kOutput, calls=%fused_computation.18.clone.1 | convolution fusion | flops 557838336 | bytes 35684356 | tf_op jit(solution)/shard_map/while/body/eval_jaxpr/while/body/eval_jaxpr/qhd,khd->hqk/dot_general | solution.py:27
  579.0 11.4 %multiply_reduce_fusion.5 = (f32[8,512]{1,0:T(8,128)}, f32[8,512,1024]{2,1,0:T(8,128)}) fusion(f32[8,512,1024]{2,1,0:T(8,128)S(1)} %fusion.125, f32[8,512]{1,0:T(8,128)} %dynamic-slice_bitcast_fusion.2, bf16[1024,8,64]{0,2,1:T(8,128)(2,1)S(1)} %get-tuple-element.441, bf16[1024,8,64]{0,2,1:T(8,128)(2,1)} %get-tuple-element.440, s32[]{:T(128)S(6)} %select_n.57, ...), kind=kOutput, calls=%fused_computation.18.clone.1 | convolution fusion | flops 557838336 | bytes 35684356 | tf_op jit(solution)/shard_map/while/body/eval_jaxpr/while/body/eval_jaxpr/qhd,khd->hqk/dot_general | solution.py:27
  632.3 12.0 %fusion.51 = f32[2048,1024]{0,1:T(8,128)} fusion(bf16[1024,1024]{1,0:T(8,128)(2,1)} %all-gather.21.cloned.1.call-done, f32[1024,2048]{1,0:T(8,128)} %fusion.60, f32[2048]{0:T(1024)S(1)} %copy-done.43), kind=kOutput, calls=%fused_computation.105 | convolution fusion | flops 4315938816 | bytes 18882560 | tf_op jit(solution)/shard_map/rf,rd->fd/dot_general | solution.py:187
  670.8 15.2 %reduce-scatter.15.cloned.1.call-done = f32[512,1024]{1,0:T(8,128)} async-done(((f32[1024,1024]{1,0:T(8,128)}), f32[512,1024]{1,0:T(8,128)}) %reduce-scatter.15.cloned.1.call-update) | async-done | bytes 2097168 | tf_op jit(solution)/shard_map/reduce_scatter | solution.py:219
  691.8 40.2 %all-reduce = (f32[6,1024]{1,0:T(8,128)S(1)}, f32[2,1024]{1,0:T(2,128)S(1)}, f32[4096]{0:T(1024)S(1)}) all-reduce(f32[6,1024]{1,0:T(8,128)S(1)} %stack.38, f32[2,1024]{1,0:T(2,128)S(1)} %maximum_dynamic-update-slice_fusion, f32[4096]{0:T(1024)S(1)} %dynamic_update_slice.30), channel_id=1, replica_groups=mesh['dp'=16,'tensor'=2] {'dp','tensor'}, use_global_device_ids=true, to_apply=%region_25.26 | all-reduce | flops 12288 | bytes 98304 | tf_op jit(solution)/shard_map/psum | solution.py:247
  733.8 61.5 %reduce-scatter.23.cloned.1.call-done = f32[2048,64]{0,1:T(8,128)} async-done(((f32[2048,1024]{0,1:T(8,128)}), f32[2048,64]{0,1:T(8,128)}) %reduce-scatter.23.cloned.1.call-update) | async-done | bytes 524304 | tf_op jit(solution)/shard_map/reduce_scatter | solution.py:229
  795.3 108.9 %reduce-scatter.21.cloned.1.call-done = f32[64,2048]{1,0:T(8,128)} async-done(((f32[1024,2048]{1,0:T(8,128)}), f32[64,2048]{1,0:T(8,128)}) %reduce-scatter.21.cloned.1.call-update) | async-done | bytes 524304 | tf_op jit(solution)/shard_map/reduce_scatter | solution.py:228
  904.2 65.5 %reduce-scatter.19.cloned.1.call-done = f32[512,64]{0,1:T(8,128)} async-done(((f32[512,1024]{0,1:T(8,128)}), f32[512,64]{0,1:T(8,128)}) %reduce-scatter.19.cloned.1.call-update) | async-done | bytes 131088 | tf_op jit(solution)/shard_map/reduce_scatter | solution.py:227
  969.7 89.2 %reduce-scatter.17.cloned.1.call-done = f32[64,1536]{1,0:T(8,128)} async-done(((f32[1024,1536]{1,0:T(8,128)}), f32[64,1536]{1,0:T(8,128)}) %reduce-scatter.17.cloned.1.call-update) | async-done | bytes 393232 | tf_op jit(solution)/shard_map/reduce_scatter | solution.py:226
  (236 shorter events, 197.0 us)
Async XLA Ops:
  7.2 41.8 %all-gather.9.cloned.1.call-start = ((), (), s32[]{:S(2)}) async-start(), calls=%async_computation.8 | async-start | bytes 3145728 | tf_op jit(solution)/shard_map/all_gather | solution.py:136
  8.7 94.0 %copy-start.23 = (f32[512]{0:T(512)}, f32[512]{0:T(512)S(1)}, u32[]{:S(2)}) copy-start(f32[512]{0:T(512)S(1)} %broadcast_multiply_fusion.1) | copy-start | bytes 6148
  13.0 83.5 %all-gather.11.cloned.1.call-start = ((), (), s32[]{:S(2)}) async-start(), calls=%async_computation.9 | async-start | bytes 3342336 | tf_op jit(solution)/shard_map/all_gather | solution.py:131
  13.8 123.1 %all-gather.13.cloned.1.call-start = ((), (), s32[]{:S(2)}) async-start(), calls=%async_computation.10 | async-start | bytes 1114112 | tf_op jit(solution)/shard_map/all_gather | solution.py:132
  14.5 181.2 %reduce-scatter.9.cloned.1.call-start = ((), (), s32[]{:S(2)}) async-start(), calls=%async_computation.11 | async-start | bytes 6291456 | tf_op jit(solution)/shard_map/reduce_scatter | solution.py:162
  142.4 53.3 %copy-start.6 = (bf16[512,1024]{1,0:T(8,128)(2,1)S(1)}, bf16[512,1024]{1,0:T(8,128)(2,1)}, u32[]{:S(2)}) copy-start(bf16[512,1024]{1,0:T(8,128)(2,1)} %param.18) | copy-start | bytes 3145732
  142.4 53.3 %copy-start.39 = (f32[1024]{0:T(1024)S(1)}, f32[1024]{0:T(1024)}, u32[]{:S(2)}) copy-start(f32[1024]{0:T(1024)} %param.24) | copy-start | bytes 12292
  142.4 106.1 %all-gather.17.cloned.1.call-start = ((), (), s32[]{:S(2)}) async-start(), calls=%async_computation.13 | async-start | bytes 4456448 | tf_op jit(solution)/shard_map/all_gather | solution.py:133
  143.0 55.9 %copy-start.26 = (f32[1024]{0:T(1024)S(1)}, f32[1024]{0:T(1024)}, u32[]{:S(2)}) copy-start(f32[1024]{0:T(1024)} %param.25) | copy-start | bytes 12292
  143.0 55.9 %copy-start.36 = (f32[1024]{0:T(1024)S(1)}, f32[1024]{0:T(1024)}, u32[]{:S(2)}) copy-start(f32[1024]{0:T(1024)} %param.26) | copy-start | bytes 12292
  143.0 139.2 %all-gather.15.cloned.1.call-start = ((), (), s32[]{:S(2)}) async-start(), calls=%async_computation.12 | async-start | bytes 3145728 | tf_op jit(solution)/shard_map/all_gather | solution.py:166
  200.4 116.6 %all-gather.21.cloned.1.call-start = ((), (), s32[]{:S(2)}) async-start(), calls=%async_computation.16 | async-start | bytes 3145728 | tf_op jit(solution)/shard_map/all_gather | solution.py:185
  201.1 168.8 %all-gather.19.cloned.1.call-start = ((), (), s32[]{:S(2)}) async-start(), calls=%async_computation.14 | async-start | bytes 4456448 | tf_op jit(solution)/shard_map/all_gather | solution.py:134
  201.9 168.1 %copy-start.42 = (f32[2048]{0:T(1024)S(1)}, f32[2048]{0:T(1024)}, u32[]{:S(2)}) copy-start(f32[2048]{0:T(1024)} %param.28) | copy-start | bytes 24580
  201.9 243.0 %reduce-scatter.13.cloned.1.call-start = ((), (), s32[]{:S(2)}) async-start(), calls=%async_computation.17 | async-start | bytes 6291456 | tf_op jit(solution)/shard_map/reduce_scatter | solution.py:192
  391.9 86.9 %reduce-scatter.11.cloned.1.call-start = ((), (), s32[]{:S(2)}) async-start(), calls=%async_computation.15 | async-start | bytes 3145728 | tf_op jit(solution)/shard_map/reduce_scatter | solution.py:174
  404.2 74.6 %copy-start.37 = (f32[1024]{0:T(1024)S(1)}, f32[1024]{0:T(1024)}, u32[]{:S(2)}) copy-start(f32[1024]{0:T(1024)} %param.30) | copy-start | bytes 12292
  404.2 114.8 %all-gather.23.cloned.1.call-start = ((), (), s32[]{:S(2)}) async-start(), calls=%async_computation.18 | async-start | bytes 3145728 | tf_op jit(solution)/shard_map/all_gather | solution.py:198
  448.4 36.0 %copy-start.12 = (bf16[512,1024]{1,0:T(8,128)(2,1)S(1)}, bf16[512,1024]{1,0:T(8,128)(2,1)}, u32[]{:S(2)}) copy-start(bf16[512,1024]{1,0:T(8,128)(2,1)} %param.31) | copy-start | bytes 3145732
  485.7 200.3 %reduce-scatter.15.cloned.1.call-start = ((), (), s32[]{:S(2)}) async-start(), calls=%async_computation.19 | async-start | bytes 6291456 | tf_op jit(solution)/shard_map/reduce_scatter | solution.py:219
  631.6 163.7 %reduce-scatter.23.cloned.1.call-start = ((), (), s32[]{:S(2)}) async-start(), calls=%async_computation.23 | async-start | bytes 8912896 | tf_op jit(solution)/shard_map/reduce_scatter | solution.py:229
  644.3 259.9 %reduce-scatter.21.cloned.1.call-start = ((), (), s32[]{:S(2)}) async-start(), calls=%async_computation.22 | async-start | bytes 8912896 | tf_op jit(solution)/shard_map/reduce_scatter | solution.py:228
  655.4 314.3 %reduce-scatter.19.cloned.1.call-start = ((), (), s32[]{:S(2)}) async-start(), calls=%async_computation.21 | async-start | bytes 2228224 | tf_op jit(solution)/shard_map/reduce_scatter | solution.py:227
  660.9 398.0 %reduce-scatter.17.cloned.1.call-start = ((), (), s32[]{:S(2)}) async-start(), calls=%async_computation.20 | async-start | bytes 6684672 | tf_op jit(solution)/shard_map/reduce_scatter | solution.py:226
  (47 other events, 288.6 us)
Sparse Core Ops, SparseCore 0:
  13.2 35.8 all-gather.8
  51.3 45.1 all-gather.10
  98.7 36.7 all-gather.12
  142.5 53.1 reduce-scatter.8
  197.9 50.5 all-gather.16
  250.6 31.6 all-gather.14
  283.8 33.1 all-gather.20
  319.4 50.5 all-gather.18
  392.0 52.7 reduce-scatter.12
  446.9 31.8 reduce-scatter.10
  485.9 33.1 all-gather.22
  631.7 54.2 reduce-scatter.14
  690.7 104.5 reduce-scatter.22
  799.8 104.3 reduce-scatter.20
  908.4 61.2 reduce-scatter.18
  974.6 84.2 reduce-scatter.16
where the time goes:
time: 1070 us
  waiting for transfers between devices  739 us (69%)
  matrix products  177 us (17%)
  other arithmetic  59.3 us (6%)
  blocking collectives  40.2 us (4%)
  local copies, waits for them, and re-layouts  26.5 us (2%)
  between operations  14.8 us (1%)
    reduce_scatter x1, waiting for transfers between devices, body(): lax.psum_scatter(grad_fc1, 'dp', scatter_dimension=0, tiled=True)  109 us
    reduce_scatter x1, waiting for transfers between devices, body(): lax.psum_scatter(grad_qkv_w, 'dp', scatter_dimension=0, tiled=True)  89.2 us
    reduce_scatter x1, waiting for transfers between devices, body(): lax.psum_scatter(grad_out_w, 'dp', scatter_dimension=1, tiled=True)  65.5 us
    reduce_scatter x1, waiting for transfers between devices, body(): lax.psum_scatter(grad_fc2, 'dp', scatter_dimension=1, tiled=True)  61.5 us
    all_gather x1, waiting for transfers between devices, body(): lax.all_gather(fc2_weight, 'dp', axis=1, tiled=True)  53 us
    reduce_scatter x1, waiting for transfers between devices, body(): lax.psum_scatter(row_product(context, out_full), 'tensor', scatter_dimens...  52.6 us
    all_gather x1, waiting for transfers between devices, body(): lax.all_gather(qkv_weight, 'dp', axis=0, tiled=True)  47.5 us
    all_gather x1, waiting for transfers between devices, body(): lax.all_gather(fc1_weight, 'dp', axis=0, tiled=True)  46.3 us
  transfers between devices with their start and end apart: 16, of which 15 were waited for; matrix products, arithmetic and copies ran while one was open for 11% of the time, Pallas kernels for 0%

commit v1 on v0

--- a/solution.py
+++ b/solution.py
@@ -3,6 +3,9 @@
 import jax
 import jax.numpy as jnp
 from jax import lax
+from jax.experimental import pallas as pl
+from jax.experimental.pallas import tpu as pltpu
+from jax.sharding import Mesh
 from jax.sharding import PartitionSpec as P
 
 D = 1024
@@ -265,7 +268,339 @@
     )
 
 
+ALL = ("zx", "core", "tensor")
+GROUP = ("zx", "tensor")
+NEG = -1e30
+
+
+def natural_rows(ref, first, second, half):
+    return jnp.concatenate([ref[pl.ds(first, half), :], ref[pl.ds(second, half), :]], 0)
+
+
+def half_offsets(index_ref, half):
+    index = index_ref[0]
+    return pl.multiple_of(index * half, half), pl.multiple_of((1 - index) * half, half)
+
+
+def dot_nt(left, right):
+    return lax.dot_general(left, right, (((1,), (1,)), ((), ())), preferred_element_type=jnp.float32)
+
+
+def dot_tn(left, right):
+    return lax.dot_general(left, right, (((0,), (0,)), ((), ())), preferred_element_type=jnp.float32)
+
+
+def block_probs(query_rows, keys, block):
+    scores = dot_nt(query_rows, keys)
+    before = keys.shape[0] - block
+    rows = lax.broadcasted_iota(jnp.int32, (block, block), 0)
+    columns = lax.broadcasted_iota(jnp.int32, (block, block), 1)
+    diagonal = jnp.where(columns <= rows, scores[:, before:], NEG)
+    if before:
+        scores = jnp.concatenate([scores[:, :before], diagonal], 1)
+    else:
+        scores = diagonal
+    expo = jnp.exp(scores - jnp.max(scores, -1, keepdims=True))
+    return expo * (1.0 / jnp.sum(expo, -1, keepdims=True))
+
+
+def attend_kernel(index_ref, qkv_ref, context_ref):
+    half = qkv_ref.shape[0] // 2
+    block = half // 2
+    first, second = half_offsets(index_ref, half)
+    qkv = natural_rows(qkv_ref, first, second, half)
+    heads = qkv.shape[1] // (3 * HD)
+    for i in range(4):
+        row = (first if i < 2 else second) + (i % 2) * block
+        parts = []
+        for h in range(heads):
+            base = h * 3 * HD
+            query_rows = qkv[i * block : (i + 1) * block, base : base + HD] * HD ** (-0.5)
+            keys = qkv[: (i + 1) * block, base + HD : base + 2 * HD]
+            values = qkv[: (i + 1) * block, base + 2 * HD : base + 3 * HD]
+            probs = block_probs(query_rows.astype(jnp.bfloat16), keys, block)
+            parts.append(
+                jnp.dot(probs.astype(jnp.bfloat16), values, preferred_element_type=jnp.float32)
+            )
+        context_ref[pl.ds(pl.multiple_of(row, block), block), :] = jnp.concatenate(
+            parts, 1
+        ).astype(jnp.bfloat16)
+
+
+def attend_back_kernel(index_ref, qkv_ref, grad_ref, out_ref):
+    half = qkv_ref.shape[0] // 2
+    block = half // 2
+    first, second = half_offsets(index_ref, half)
+    qkv = natural_rows(qkv_ref, first, second, half)
+    grad = natural_rows(grad_ref, first, second, half)
+    heads = qkv.shape[1] // (3 * HD)
+    starts = [
+        pl.multiple_of((first if i < 2 else second) + (i % 2) * block, block) for i in range(4)
+    ]
+    for h in range(heads):
+        base = h * 3 * HD
+        queries = (qkv[:, base : base + HD] * HD ** (-0.5)).astype(jnp.bfloat16)
+        keys = qkv[:, base + HD : base + 2 * HD]
+        values = qkv[:, base + 2 * HD : base + 3 * HD]
+        grad_head = grad[:, h * HD : (h + 1) * HD]
+        grad_keys = [None] * 4
+        grad_values = [None] * 4
+        for i in range(4):
+            rows = slice(i * block, (i + 1) * block)
+            seen = slice(0, (i + 1) * block)
+            probs = block_probs(queries[rows], keys[seen], block)
+            grad_probs = dot_nt(grad_head[rows], values[seen])
+            inner = jnp.sum(probs * grad_probs, -1, keepdims=True)
+            grad_scores = (probs * (grad_probs - inner)).astype(jnp.bfloat16)
+            grad_query = jnp.dot(grad_scores, keys[seen], preferred_element_type=jnp.float32)
+            out_ref[pl.ds(starts[i], block), base : base + HD] = (
+                grad_query * HD ** (-0.5)
+            ).astype(jnp.bfloat16)
+            key_term = dot_tn(grad_scores, queries[rows])
+            value_term = dot_tn(probs.astype(jnp.bfloat16), grad_head[rows])
+            for j in range(i + 1):
+                key_part = key_term[j * block : (j + 1) * block]
+                value_part = value_term[j * block : (j + 1) * block]
+                grad_keys[j] = key_part if i == j else grad_keys[j] + key_part
+                grad_values[j] = value_part if i == j else grad_values[j] + value_part
+        for j in range(4):
+            out_ref[pl.ds(starts[j], block), base + HD : base + 3 * HD] = jnp.concatenate(
+                [grad_keys[j], grad_values[j]], 1
+            ).astype(jnp.bfloat16)
+
+
+def attend(index, qkv):
+    rows, width = qkv.shape
+    pairs = width // (6 * HD)
+    return pl.pallas_call(
+        attend_kernel,
+        grid=(pairs,),
+        in_specs=[
+            pl.BlockSpec(memory_space=pltpu.SMEM),
+            pl.BlockSpec((rows, 6 * HD), lambda i: (0, i)),
+        ],
+        out_specs=pl.BlockSpec((rows, 2 * HD), lambda i: (0, i)),
+        out_shape=jax.ShapeDtypeStruct((rows, width // 3), jnp.bfloat16),
+        compiler_params=pltpu.CompilerParams(vmem_limit_bytes=40 << 20),
+        cost_estimate=pl.CostEstimate(
+            flops=pairs * 8 * HD * rows * rows,
+            bytes_accessed=8 * rows * width // 3,
+            transcendentals=pairs * 2 * rows * rows,
+        ),
+    )(index, qkv)
+
+
+def attend_back(index, qkv, grad):
+    rows, width = qkv.shape
+    pairs = width // (6 * HD)
+    return pl.pallas_call(
+        attend_back_kernel,
+        grid=(pairs,),
+        in_specs=[
+            pl.BlockSpec(memory_space=pltpu.SMEM),
+            pl.BlockSpec((rows, 6 * HD), lambda i: (0, i)),
+            pl.BlockSpec((rows, 2 * HD), lambda i: (0, i)),
+        ],
+        out_specs=pl.BlockSpec((rows, 6 * HD), lambda i: (0, i)),
+        out_shape=jax.ShapeDtypeStruct((rows, width), jnp.bfloat16),
+        compiler_params=pltpu.CompilerParams(vmem_limit_bytes=40 << 20),
+        cost_estimate=pl.CostEstimate(
+            flops=pairs * 20 * HD * rows * rows,
+            bytes_accessed=14 * rows * width // 3,
+            transcendentals=pairs * 2 * rows * rows,
+        ),
+    )(index, qkv, grad)
+
+
+def pair_body(
+    zx_size,
+    inputs,
+    norm1_gain,
+    norm1_bias,
+    qkv_weight,
+    qv_bias,
+    out_weight,
+    out_bias,
+    norm2_gain,
+    norm2_bias,
+    fc1_weight,
+    fc1_bias,
+    fc2_weight,
+    fc2_bias,
+    cotangent,
+):
+    f32, bf16 = jnp.float32, jnp.bfloat16
+    crossing = [
+        (z * 4 + c * 2 + t, z * 4 + t * 2 + c)
+        for z in range(zx_size)
+        for c in range(2)
+        for t in range(2)
+    ]
+
+    def swap(value):
+        return lax.ppermute(value, ALL, crossing)
+
+    def flip(value):
+        return lax.ppermute(value, "core", [(0, 1), (1, 0)])
+
+    def both(own):
+        return jnp.concatenate([own, flip(own)], 0)
+
+    def pair_sum(product, rows):
+        half = rows.shape[0] // 2
+        arrived = flip(product(rows[half:]).astype(bf16))
+        return product(rows[:half]) + arrived.astype(f32)
+
+    def gather(weight, axis):
+        return lax.all_gather(weight, GROUP, axis=axis, tiled=True)
+
+    def scatter(grad, axis):
+        return lax.psum_scatter(grad.astype(bf16), GROUP, scatter_dimension=axis, tiled=True)
+
+    inputs = swap(inputs)
+    qkv_full = gather(swap(qkv_weight), 0)
+    qv_bias = swap(qv_bias)
+    fc1_bias = swap(fc1_bias)
+    out_full = gather(swap(out_weight), 1)
+    fc1_full = gather(swap(fc1_weight), 0)
+    fc2_full = gather(swap(fc2_weight), 1)
+    cotangent = swap(cotangent)
+
+    width_here = qv_bias.shape[1]
+    heads_here = width_here // HD
+    inputs_f = inputs.astype(f32)
+    index = lax.axis_index("core").astype(jnp.int32).reshape(1)
+    normed1 = both(layer_norm(inputs_f, norm1_gain, norm1_bias).astype(bf16))
+    head_bias = jnp.stack(
+        [
+            qv_bias[0].reshape(heads_here, HD),
+            jnp.zeros((heads_here, HD), f32),
+            qv_bias[1].reshape(heads_here, HD),
+        ],
+        1,
+    ).reshape(3 * width_here)
+    qkv = (row_product(normed1, qkv_full) + head_bias).astype(bf16)
+    context = attend(index, qkv)
+    middle = inputs_f + pair_sum(lambda rows: row_product(rows, out_full), context) + out_bias
+    normed2 = both(layer_norm(middle, norm2_gain, norm2_bias).astype(bf16))
+    pre_act = row_product(normed2, fc1_full) + fc1_bias
+    activ = jax.nn.gelu(pre_act, approximate=True).astype(bf16)
+    branch = pair_sum(lambda rows: row_product(rows, fc2_full), activ)
+    outputs = swap((middle + branch + fc2_bias).astype(bf16))
+
+    grad_outputs = cotangent.astype(f32)
+    grad_branch = both(cotangent)
+    grad_fc2 = swap(
+        scatter(jnp.einsum("rf,rd->fd", activ, grad_branch, preferred_element_type=f32), 1)
+    ).astype(f32)
+    grad_activ = row_product_back(grad_branch, fc2_full)
+    gelu_pull = jax.vjp(partial(jax.nn.gelu, approximate=True), pre_act)[1]
+    grad_pre = gelu_pull(grad_activ)[0].astype(bf16)
+    grad_fc1_b = jnp.sum(grad_pre.astype(f32), 0)
+    grad_fc1 = swap(
+        scatter(jnp.einsum("rd,rf->df", normed2, grad_pre, preferred_element_type=f32), 0)
+    ).astype(f32)
+    grad_normed2 = pair_sum(lambda rows: row_product_back(rows, fc1_full), grad_pre)
+    norm2_pull = jax.vjp(layer_norm, middle, norm2_gain, norm2_bias)[1]
+    grad_mid_norm, grad_gain2, grad_shift2 = norm2_pull(grad_normed2)
+    grad_middle = grad_outputs + grad_mid_norm
+    grad_attn = both(grad_middle.astype(bf16))
+    grad_ctx = row_product_back(grad_attn, out_full).astype(bf16)
+    grad_out = swap(
+        scatter(jnp.einsum("rc,rd->cd", context, grad_attn, preferred_element_type=f32), 1)
+    ).astype(f32)
+    grad_proj = attend_back(index, qkv, grad_ctx)
+    grad_bias = jnp.sum(grad_proj.astype(f32), 0).reshape(heads_here, 3, HD)
+    grad_qkv = swap(
+        scatter(jnp.einsum("rd,rc->dc", normed1, grad_proj, preferred_element_type=f32), 0)
+    ).astype(f32)
+    grad_normed1 = pair_sum(lambda rows: row_product_back(rows, qkv_full), grad_proj)
+    norm1_pull = jax.vjp(layer_norm, inputs_f, norm1_gain, norm1_bias)[1]
+    grad_in_norm, grad_gain1, grad_shift1 = norm1_pull(grad_normed1)
+    grad_inputs = swap((grad_middle + grad_in_norm).astype(bf16)).astype(f32)
+
+    vectors = [
+        grad_gain1,
+        grad_shift1,
+        grad_gain2,
+        grad_shift2,
+        jnp.sum(grad_middle, 0),
+        jnp.sum(grad_outputs, 0),
+    ]
+    width = inputs.shape[1]
+    hidden = grad_fc1_b.shape[0]
+    terms = jnp.concatenate(
+        vectors + [grad_bias[:, 0].reshape(-1), grad_bias[:, 2].reshape(-1), grad_fc1_b]
+    )
+    gathered = lax.all_gather(terms, ALL, axis=0, tiled=False)
+    gathered = gathered.reshape(zx_size, 2, 2, terms.shape[0])
+    common = jnp.sum(gathered[..., : 6 * width], (0, 1, 2)).reshape(6, width)
+    halves = jnp.sum(gathered[..., 6 * width :], (0, 2))
+    mine = lax.dynamic_index_in_dim(halves, lax.axis_index("tensor"), 0, False)
+    return (
+        outputs,
+        grad_inputs,
+        common[0],
+        common[1],
+        grad_qkv,
+        mine[: 2 * width_here].reshape(2, width_here),
+        grad_out,
+        common[4],
+        common[2],
+        common[3],
+        grad_fc1,
+        mine[2 * width_here : 2 * width_here + hidden],
+        grad_fc2,
+        common[5],
+    )
+
+
+def pair_solution(mesh):
+    zx_size = mesh.shape["dp"] // 2
+    split = Mesh(mesh.devices.reshape(zx_size, 2, 2), ALL)
+    rows, spread = P(ALL, None), ("zx", "core")
+    return jax.shard_map(
+        partial(pair_body, zx_size),
+        mesh=split,
+        in_specs=(
+            rows,
+            P(),
+            P(),
+            P(spread, "tensor"),
+            P(None, "tensor"),
+            P("tensor", spread),
+            P(),
+            P(),
+            P(),
+            P(spread, "tensor"),
+            P("tensor"),
+            P("tensor", spread),
+            P(),
+            rows,
+        ),
+        out_specs=(
+            rows,
+            rows,
+            P(),
+            P(),
+            P(spread, "tensor"),
+            P(None, "tensor"),
+            P("tensor", spread),
+            P(),
+            P(),
+            P(),
+            P(spread, "tensor"),
+            P("tensor"),
+            P("tensor", spread),
+            P(),
+        ),
+        check_vma=False,
+    )
+
+
 def solution(mesh):
+    if mesh.shape["tensor"] == 2 and mesh.shape["dp"] % 2 == 0:
+        return pair_solution(mesh)
     placed = (
         P(("dp", "tensor"), None),
         P(),

time: 1070 us -> 855 us (0.80)
  waiting for transfers between devices: 739 us -> 608 us
  matrix products: 177 us -> 84.3 us
  starting transfers between devices: 1.62 us -> 61 us
  Pallas kernels: 0 us -> 47.9 us
  other arithmetic: 59.3 us -> 11.5 us
  blocking collectives: 40.2 us -> 0 us
  local copies, waits for them, and re-layouts: 26.5 us -> 15 us
    dot_general x22 -> x4, matrix products: 150 us -> 27.7 us  [the longest x1 9.41 us: pair_body(): jnp.einsum('rf,rd->fd', activ, grad_branch, preferred_element_type=f32)]
    reduce_scatter x8 -> x4, waiting for transfers between devices: 464 us -> 348 us  [scatter(): lax.psum_scatter(grad.astype(bf16), GROUP, scatter_dimension=axis, tiled=...]
    ppermute x0 -> x22, starting transfers between devices: none -> 60 us  [the longest x8 39.4 us: flip(): return lax.ppermute(value, 'core', [(0, 1), (1, 0)])]
    pallas_call x0 -> x2, Pallas kernels: none -> 47.9 us  [the longest x1 30.5 us: attend_back(): pl.pallas_call(attend_back_kernel, grid=(pairs,), in_specs=[pl.BlockSpec(...]
    psum x1 -> x0, blocking collectives: 40.2 us -> none  [body(): lax.psum((vector_terms, qv_whole, fc1_whole), ('dp', 'tensor'))]
    all_gather x8 -> x5, waiting for transfers between devices: 272 us -> 250 us  [the longest x4 199 us: gather(): return lax.all_gather(weight, GROUP, axis=axis, tiled=True)]
    convert_element_type x6 -> x8, other arithmetic: 24.5 us -> 5.85 us  [the longest x1 1.57 us: pair_body(): grad_inputs = swap((grad_middle + grad_in_norm).astype(bf16)).astype(f32)]
    dot_general x2 -> x6, matrix products: 11.2 us -> 29.1 us  [row_product_back(): jnp.einsum('rc,dc->rd', left_rows, right_mat, preferred_element_type=jnp....]
  transfers between devices with their start and end apart: 16 -> 31, of which waited for: 15 -> 13; matrix products, arithmetic and copies ran while one was open for 11% -> 9% of each run, Pallas kernels for 0% -> 2%
where the time goes in v1:
time: 855 us; the launch traced here: 842 us
  waiting for transfers between devices  608 us (71%)
  matrix products  84.3 us (10%)
  starting transfers between devices  61 us (7%)
  Pallas kernels  47.9 us (6%)
  local copies, waits for them, and re-layouts  15 us (2%)
  between operations  14.6 us (2%)
  other arithmetic  11.5 us (1%)
    reduce_scatter x4, waiting for transfers between devices, scatter(): lax.psum_scatter(grad.astype(bf16), GROUP, scatter_dimension=axis, tiled=...  348 us
    all_gather x4, waiting for transfers between devices, gather(): return lax.all_gather(weight, GROUP, axis=axis, tiled=True)  199 us
    all_gather x1, waiting for transfers between devices, pair_body(): gathered = lax.all_gather(terms, ALL, axis=0, tiled=False)  50.6 us
    ppermute x8, starting transfers between devices, flip(): return lax.ppermute(value, 'core', [(0, 1), (1, 0)])  39.4 us
    pallas_call x1, Pallas kernels, attend_back(): pl.pallas_call(attend_back_kernel, grid=(pairs,), in_specs=[pl.BlockSpec(...  30.5 us
    dot_general x6, matrix products, row_product_back(): jnp.einsum('rc,dc->rd', left_rows, right_mat, preferred_element_type=jnp....  29.1 us
    dot_general x6, matrix products, row_product(): return jnp.dot(left_rows, right_mat, preferred_element_type=jnp.float32)  27.5 us
    ppermute x14, starting transfers between devices, swap(): return lax.ppermute(value, ALL, crossing)  20.7 us
  transfers between devices with their start and end apart: 31, of which 13 were waited for; matrix products, arithmetic and copies ran while one was open for 9% of the time, Pallas kernels for 2%

profile of v1, /device:TPU:0, one launch (start us, length us, event | category | flops | bytes accessed | tf_op | source)
XLA Modules:
  0.0 841.8 jit_solution(13873739951536788510)
XLA Ops:
  19.6 37.9 %collective-permute-start.1 = (bf16[512,1024]{1,0:T(8,128)(2,1)S(1)}, bf16[512,1024]{1,0:T(8,128)(2,1)}, u32[]{:S(2)}, u32[]{:S(2)}) collective-permute-start(bf16[512,1024]{1,0:T(8,128)(2,1)S(1)} %fusion.14), channel_id=1, source_target_pairs={{0,2},{2,0},{1,3},{3,1},{4,6},{6,4},{5,7},{7,5},{8,10},{10,8},{9,1... | collective-permute-start | bytes 3145736 | tf_op jit(solution)/shard_map/ppermute | solution.py:444
  60.4 32.0 %all-gather.7.cloned.1.call-done = bf16[1024,1536]{1,0:T(8,128)(2,1)} async-done(((bf16[64,1536]{1,0:T(8,128)(2,1)}), bf16[1024,1536]{1,0:T(8,128)(2,1)}) %all-gather.7.cloned.1.call-update) | async-done | bytes 3145744 | tf_op jit(solution)/shard_map/all_gather | solution.py:455
  92.4 5.6 add_convert_fusion.qkv_ref
  98.0 17.4 %shard_map.245 = bf16[1024,512]{1,0:T(8,128)(2,1)S(1)} custom-call(s32[1]{0:T(128)} %bitcast.index_ref, bf16[1024,1536]{1,0:T(8,128)(2,1)S(1)} %add_convert_fusion.qkv_ref), custom_call_target="tpu_custom_call" | custom-call | flops 2147483648 | bytes 4194304 | tf_op jit(solution)/shard_map/pallas_call | solution.py:375
  117.2 32.3 %all-gather.9.cloned.1.call-done = bf16[512,1024]{0,1:T(8,128)(2,1)} async-done(((bf16[512,64]{0,1:T(8,128)(2,1)}), bf16[512,1024]{0,1:T(8,128)(2,1)}) %all-gather.9.cloned.1.call-update) | async-done | bytes 1048592 | tf_op jit(solution)/shard_map/all_gather | solution.py:455
  160.0 67.5 %all-gather.11.cloned.1.call-done = bf16[1024,2048]{1,0:T(8,128)(2,1)} async-done(((bf16[64,2048]{1,0:T(8,128)(2,1)}), bf16[1024,2048]{1,0:T(8,128)(2,1)}) %all-gather.11.cloned.1.call-update) | async-done | bytes 4194320 | tf_op jit(solution)/shard_map/all_gather | solution.py:455
  227.5 10.1 %fusion.46 = f32[1024,2048]{1,0:T(8,128)} fusion(bf16[1024,2048]{1,0:T(8,128)(2,1)} %all-gather.11.cloned.1.call-done, bf16[512,1024]{1,0:T(8,128)(2,1)S(1)} %collective-permute-done.6, bf16[512,1024]{1,0:T(8,128)(2,1)S(1)} %add_convert_fusion.3), kind=kOutput, calls=%fused_computation.64 | convolution fusion | flops 4299161600 | bytes 14680064 | tf_op jit(solution)/shard_map/dot_general | solution.py:104
  237.6 67.7 %all-gather.13.cloned.1.call-done = bf16[2048,1024]{0,1:T(8,128)(2,1)} async-done(((bf16[2048,64]{0,1:T(8,128)(2,1)}), bf16[2048,1024]{0,1:T(8,128)(2,1)}) %all-gather.13.cloned.1.call-update) | async-done | bytes 4194320 | tf_op jit(solution)/shard_map/all_gather | solution.py:455
  305.2 15.0 %convert_reduce_fusion = (f32[2048]{0:T(1024)S(1)}, bf16[1024,2048]{1,0:T(8,128)(2,1)S(1)}, bf16[1024,2048]{1,0:T(8,128)(2,1)}) fusion(f32[1024,2048]{1,0:T(8,128)} %fusion.46, f32[2048]{0:T(1024)S(1)} %collective-permute-done.8, bf16[1024,1024]{1,0:T(8,128)(2,1)} %constant_dynamic-update-slice_fusion, bf16[2048,1024]{0,1:T(8,128)(2,1)} %all-gather.13.cloned.1.call-done), kind=kOutput, calls=%fused_computation.9 | convolution fusion | flops 4347394048 | bytes 23085056 | tf_op jit(solution)/shard_map/rc,dc->rd/dot_general | solution.py:108
  322.7 2.6 collective-permute-done.14
  325.4 3.0 multiply_reduce_fusion
  334.4 30.5 %shard_map.246 = bf16[1024,1536]{1,0:T(8,128)(2,1)S(1)} custom-call(s32[1]{0:T(128)} %bitcast.index_ref, bf16[1024,1536]{1,0:T(8,128)(2,1)S(1)} %copy-done.3, bf16[1024,512]{1,0:T(8,128)(2,1)S(1)} %convolution_convert_fusion.4.grad_ref), custom_call_target="tpu_custom_call" | custom-call | flops 5368709120 | bytes 7340032 | tf_op jit(solution)/shard_map/pallas_call | solution.py:396
  364.9 2.9 fusion.37
  371.4 4.6 fusion.60
  380.7 9.4 %convolution_convert_fusion.2 = bf16[1024,2048]{1,0:T(8,128)(2,1)} fusion(bf16[1024,2048]{1,0:T(8,128)(2,1)} %copy-done.36, bf16[512,1024]{1,0:T(8,128)(2,1)} %copy-done.30, bf16[512,1024]{1,0:T(8,128)(2,1)} %copy-done.14), kind=kOutput, calls=%fused_computation.15 | convolution fusion | flops 4301258752 | bytes 10485760 | tf_op jit(solution)/shard_map/rd,rf->df/dot_general | solution.py:501
  390.4 9.4 %convolution_convert_fusion.1 = bf16[2048,1024]{0,1:T(8,128)(2,1)} fusion(bf16[1024,2048]{1,0:T(8,128)(2,1)} %get-tuple-element.31, bf16[1024,1024]{1,0:T(8,128)(2,1)} %constant_dynamic-update-slice_fusion), kind=kOutput, calls=%fused_computation.14 | convolution fusion | flops 4297064448 | bytes 10485760 | tf_op jit(solution)/shard_map/rf,rd->fd/dot_general | solution.py:494
  399.9 6.6 convolution_convert_fusion
  406.5 5.3 fusion.40
  414.6 3.5 add_convert_fusion.2
  420.7 26.3 %reduce-scatter.7.cloned.1.call-done = bf16[512,64]{0,1:T(8,128)(2,1)} async-done(((bf16[512,1024]{0,1:T(8,128)(2,1)}), bf16[512,64]{0,1:T(8,128)(2,1)}) %reduce-scatter.7.cloned.1.call-update) | async-done | bytes 65552 | tf_op jit(solution)/shard_map/reduce_scatter | solution.py:458
  450.7 50.6 %all-gather.15.cloned.1.call-done = f32[294912]{0:T(1024)} async-done(((f32[9216]{0:T(1024)}), f32[294912]{0:T(1024)}) %all-gather.15.cloned.1.call-update) | async-done | bytes 1179664 | tf_op jit(solution)/shard_map/all_gather | solution.py:535
  503.4 94.8 %reduce-scatter.9.cloned.1.call-done = bf16[64,2048]{1,0:T(8,128)(2,1)} async-done(((bf16[1024,2048]{1,0:T(8,128)(2,1)}), bf16[64,2048]{1,0:T(8,128)(2,1)}) %reduce-scatter.9.cloned.1.call-update) | async-done | bytes 262160 | tf_op jit(solution)/shard_map/reduce_scatter | solution.py:458
  599.8 94.8 %reduce-scatter.11.cloned.1.call-done = bf16[2048,64]{0,1:T(8,128)(2,1)} async-done(((bf16[2048,1024]{0,1:T(8,128)(2,1)}), bf16[2048,64]{0,1:T(8,128)(2,1)}) %reduce-scatter.11.cloned.1.call-update) | async-done | bytes 262160 | tf_op jit(solution)/shard_map/reduce_scatter | solution.py:458
  697.7 131.9 %reduce-scatter.5.cloned.1.call-done = bf16[64,1536]{1,0:T(8,128)(2,1)} async-done(((bf16[1024,1536]{1,0:T(8,128)(2,1)}), bf16[64,1536]{1,0:T(8,128)(2,1)}) %reduce-scatter.5.cloned.1.call-update) | async-done | bytes 196624 | tf_op jit(solution)/shard_map/reduce_scatter | solution.py:458
  (191 shorter events, 65.7 us)
Async XLA Ops:
  7.2 85.2 %all-gather.7.cloned.1.call-start = ((), (), s32[]{:S(2)}) async-start(), calls=%async_computation.4 | async-start | bytes 3342336 | tf_op jit(solution)/shard_map/all_gather | solution.py:455
  9.5 140.0 %all-gather.9.cloned.1.call-start = ((), (), s32[]{:S(2)}) async-start(), calls=%async_computation.5 | async-start | bytes 1114112 | tf_op jit(solution)/shard_map/all_gather | solution.py:455
  11.7 215.7 %all-gather.11.cloned.1.call-start = ((), (), s32[]{:S(2)}) async-start(), calls=%async_computation.6 | async-start | bytes 4456448 | tf_op jit(solution)/shard_map/all_gather | solution.py:455
  14.1 291.1 %all-gather.13.cloned.1.call-start = ((), (), s32[]{:S(2)}) async-start(), calls=%async_computation.7 | async-start | bytes 4456448 | tf_op jit(solution)/shard_map/all_gather | solution.py:455
  14.2 4.3 collective-permute-start
  18.4 428.5 %reduce-scatter.7.cloned.1.call-start = ((), (), s32[]{:S(2)}) async-start(), calls=%async_computation.9 | async-start | bytes 1114112 | tf_op jit(solution)/shard_map/reduce_scatter | solution.py:458
  19.6 40.8 %collective-permute-start.1 = (bf16[512,1024]{1,0:T(8,128)(2,1)S(1)}, bf16[512,1024]{1,0:T(8,128)(2,1)}, u32[]{:S(2)}, u32[]{:S(2)}) collective-permute-start(bf16[512,1024]{1,0:T(8,128)(2,1)S(1)} %fusion.14), channel_id=1, source_target_pairs={{0,2},{2,0},{1,3},{3,1},{4,6},{6,4},{5,7},{7,5},{8,10},{10,8},{9,1... | collective-permute-start | bytes 3145736 | tf_op jit(solution)/shard_map/ppermute | solution.py:444
  58.1 93.6 %collective-permute-start.12 = (bf16[512,1024]{1,0:T(8,128)(2,1)}, bf16[512,1024]{1,0:T(8,128)(2,1)S(1)}, u32[]{:S(2)}, u32[]{:S(2)}) collective-permute-start(bf16[512,1024]{1,0:T(8,128)(2,1)} %param.27), channel_id=1, source_target_pairs={{0,0},{1,2},{2,1},{3,3},{4,4},{5,6},{6,5},{7,7},{8,8},{9,10},{10,9... | collective-permute-start | bytes 3145736 | tf_op jit(solution)/shard_map/ppermute | solution.py:441
  151.6 2.7 collective-permute-start.5
  151.7 7.2 collective-permute-start.13
  156.6 70.8 %collective-permute-start.6 = (bf16[512,1024]{1,0:T(8,128)(2,1)S(1)}, bf16[512,1024]{1,0:T(8,128)(2,1)S(1)}, u32[]{:S(2)}, u32[]{:S(2)}) collective-permute-start(bf16[512,1024]{1,0:T(8,128)(2,1)S(1)} %add_convert_fusion.3), channel_id=1, source_target_pairs={{0,2},{2,0},{1,3},{3,1},{4,6},{6,4},{5,7},{7,5},{8,10},{10,8},{9,1... | collective-permute-start | bytes 3145736 | tf_op jit(solution)/shard_map/ppermute | solution.py:444
  156.8 80.8 %collective-permute-start.8 = (f32[2048]{0:T(1024)S(1)}, f32[2048]{0:T(1024)S(1)}, u32[]{:S(2)}, u32[]{:S(2)}) collective-permute-start(f32[2048]{0:T(1024)S(1)} %copy-done.31), channel_id=1, source_target_pairs={{0,0},{1,2},{2,1},{3,3},{4,4},{5,6},{6,5},{7,7},{8,8},{9,10},{10,9... | collective-permute-start | bytes 24584 | tf_op jit(solution)/shard_map/ppermute | solution.py:441
  322.7 2.7 collective-permute-start.14
  367.7 3.7 collective-permute-start.16
  370.2 131.1 %all-gather.15.cloned.1.call-start = ((), (), s32[]{:S(2)}) async-start(), calls=%async_computation.12 | async-start | bytes 1216512 | tf_op jit(solution)/shard_map/all_gather | solution.py:535
  380.7 217.5 %reduce-scatter.9.cloned.1.call-start = ((), (), s32[]{:S(2)}) async-start(), calls=%async_computation.10 | async-start | bytes 4456448 | tf_op jit(solution)/shard_map/reduce_scatter | solution.py:458
  390.1 304.5 %reduce-scatter.11.cloned.1.call-start = ((), (), s32[]{:S(2)}) async-start(), calls=%async_computation.11 | async-start | bytes 4456448 | tf_op jit(solution)/shard_map/reduce_scatter | solution.py:458
  399.8 429.7 %reduce-scatter.5.cloned.1.call-start = ((), (), s32[]{:S(2)}) async-start(), calls=%async_computation.8 | async-start | bytes 3342336 | tf_op jit(solution)/shard_map/reduce_scatter | solution.py:458
  411.8 2.7 collective-permute-start.10
  418.1 30.4 %collective-permute-start.11 = (bf16[512,1024]{1,0:T(8,128)(2,1)}, bf16[512,1024]{1,0:T(8,128)(2,1)S(1)}, u32[]{:S(2)}, u32[]{:S(2)}) collective-permute-start(bf16[512,1024]{1,0:T(8,128)(2,1)} %add_convert_fusion.2), channel_id=1, source_target_pairs={{0,0},{1,2},{2,1},{3,3},{4,4},{5,6},{6,5},{7,7},{8,8},{9,10},{10,9... | collective-permute-start | bytes 3145736 | tf_op jit(solution)/shard_map/ppermute | solution.py:441
  419.9 28.5 %collective-permute-start.17 = (bf16[512,1024]{1,0:T(8,128)(2,1)S(1)}, bf16[512,1024]{1,0:T(8,128)(2,1)S(1)}, u32[]{:S(2)}, u32[]{:S(2)}) collective-permute-start(bf16[512,1024]{1,0:T(8,128)(2,1)S(1)} %copy-done.15), channel_id=1, source_target_pairs={{0,0},{1,2},{2,1},{3,3},{4,4},{5,6},{6,5},{7,7},{8,8},{9,10},{10,9... | collective-permute-start | bytes 3145736 | tf_op jit(solution)/shard_map/ppermute | solution.py:441
  446.9 3.1 collective-permute-start.19
  598.2 234.3 %collective-permute-start.20 = (bf16[64,2048]{1,0:T(8,128)(2,1)}, bf16[64,2048]{1,0:T(8,128)(2,1)S(1)}, u32[]{:S(2)}, u32[]{:S(2)}) collective-permute-start(bf16[64,2048]{1,0:T(8,128)(2,1)} %reduce-scatter.9.cloned.1.call-done), channel_id=1, source_target_pairs={{0,0},{1,2},{2,1},{3,3},{4,4},{5,6},{6,5},{7,7},{8,8},{9,10},{10,9... | collective-permute-start | bytes 786440 | tf_op jit(solution)/shard_map/ppermute | solution.py:441
  694.6 138.7 %collective-permute-start.21 = (bf16[2048,64]{0,1:T(8,128)(2,1)}, bf16[2048,64]{0,1:T(8,128)(2,1)S(1)}, u32[]{:S(2)}, u32[]{:S(2)}) collective-permute-start(bf16[2048,64]{0,1:T(8,128)(2,1)} %reduce-scatter.11.cloned.1.call-done), channel_id=1, source_target_pairs={{0,0},{1,2},{2,1},{3,3},{4,4},{5,6},{6,5},{7,7},{8,8},{9,10},{10,9... | collective-permute-start | bytes 786440 | tf_op jit(solution)/shard_map/ppermute | solution.py:441
  (44 other events, 755.1 us)
Sparse Core Ops, SparseCore 0:
  11.5 80.8 all-gather.6
  95.7 53.7 all-gather.8
  152.9 74.5 all-gather.10
  230.7 74.5 all-gather.12
  370.3 76.5 reduce-scatter.6
  450.7 50.5 all-gather.14
  503.7 94.4 reduce-scatter.8
  600.6 93.9 reduce-scatter.10
  700.4 129.0 reduce-scatter.4
